TPU v7x, 32 devices: a whole 2x2x4 slice. The times are simulated.
32 devices in a mesh: groups: 2 (over x), seq: 8 (over z, y), tp: 2 (over core).
Axes of the slice: x: 2, y: 2, z: 4, core: 2. Of those that a mesh axis runs over, the one named last changes fastest.
Arguments:
- token_ids: int32 [2048], P(('groups', 'seq')), parts along dimension 0, may hold values from 0 to 511
- embed_table: bfloat16 [512, 4096], P(None, 'tp'), may hold values from -4 to 4
- hyena_qkv: bfloat16 [3, 2048, 4096], P(None, ('groups', 'seq'), 'tp'), parts along dimension 1, may hold values from -5 to 5
- conv_weights: float32 [3, 3, 4096], P(None, None, 'tp'), may hold values from -2.5 to 2.5
- decay_rates: float32 [8, 4096], P(None, 'tp'), may hold values from 0 to 1, as said below
- residues: float32 [8, 4096], P(None, 'tp'), may hold values from -2 to 2
- prior_state: float32 [16, 4096], P('groups', 'tp'), parts along dimension 0, may hold values from -4 to 4
Outputs:
- hyena_out: bfloat16 [2048, 4096], P(('groups', 'seq'), 'tp'), parts along dimension 0
- end_state: float32 [16, 4096], P('groups', ('tp', 'seq')), parts along dimension 0
There are 2 independent parts, one for each index of `groups`. A program takes and returns all parts, laid end to end along the dimension named above; an argument that names none is the same for every part. Nothing has to cross between parts.
Inputs may be any that keep to these rules, and one draw needn't show every extreme that they name: `decay_rates`: decay rates of the modes, positive.
All inputs are finite; a program needn't handle non-finite values.
Results may differ from a plain program's by a relative error of at most 0.001.
Values may be sent and summed in bfloat16 or wider, within the bound.
A program may use at most 128 MiB of HBM per device.

v0:
```python
import jax
import jax.numpy as jnp
from jax import lax
from jax.sharding import PartitionSpec as P


def shifted(array, axis, by):
    size = lax.axis_size(axis)
    pairs = [(i, i + by) for i in range(size) if 0 <= i + by < size]
    return lax.ppermute(array, axis, pairs)


def short_features(extended, conv_weights, tok_local):
    tap_count = conv_weights.shape[1]
    results = []
    for member in range(3):
        total = jnp.zeros((tok_local, extended.shape[2]), jnp.float32)
        for tap_index in range(tap_count):
            offset = tap_count - 1 - tap_index
            total = total + conv_weights[member, tap_index][None, :] * extended[
                member, offset : offset + tok_local
            ].astype(jnp.float32)
        results.append(total)
    return results


def modal_local(product_in, decay_rates, residues, sub_len):
    tok_local, channels = product_in.shape
    block_count = tok_local // sub_len
    blocks = product_in.reshape(block_count, sub_len, channels)
    spacing = jnp.arange(sub_len, dtype=jnp.float32)
    gain = jnp.sqrt(-jnp.expm1(-2.0 * decay_rates))
    decay_table = jnp.exp(-decay_rates[:, None, :] * spacing[None, :, None])
    kernel = jnp.sum((residues * gain)[:, None, :] * decay_table, axis=0)
    extended = jnp.concatenate(
        [kernel[::-1], jnp.zeros((sub_len - 1, channels), jnp.float32)], axis=0
    )
    toeplitz = jnp.stack(
        [extended[sub_len - 1 - row : 2 * sub_len - 1 - row] for row in range(sub_len)], axis=0
    )
    inner = jnp.einsum("tsc,bsc->btc", toeplitz, blocks, precision=lax.Precision.HIGHEST)
    tail_weight = gain[:, None, :] * jnp.exp(
        -decay_rates[:, None, :] * (sub_len - 1 - spacing)[None, :, None]
    )
    closing = jnp.einsum("bsc,msc->bmc", blocks, tail_weight, precision=lax.Precision.HIGHEST)
    per_block = jnp.exp(-decay_rates * sub_len)

    def advance(carry, piece):
        return (per_block * carry + piece, carry)

    local_end, starts = lax.scan(advance, jnp.zeros_like(decay_rates), closing)
    return (inner, starts, local_end)


def modal_readout(inner, starts, incoming, decay_rates, residues, sub_len):
    block_count = starts.shape[0]
    block_pos = jnp.arange(block_count, dtype=jnp.float32) * sub_len
    opening = (
        starts + jnp.exp(-decay_rates[None, :, :] * block_pos[:, None, None]) * incoming[None, :, :]
    )
    spacing = jnp.arange(sub_len, dtype=jnp.float32)
    readout = residues[:, None, :] * jnp.exp(
        -decay_rates[:, None, :] * (spacing + 1.0)[None, :, None]
    )
    outer = jnp.einsum("bmc,mtc->btc", opening, readout, precision=lax.Precision.HIGHEST)
    return (inner + outer).reshape(block_count * sub_len, inner.shape[2])


def body(token_ids, embed_table, hyena_qkv, conv_weights, decay_rates, residues, prior_state):
    tok_local = hyena_qkv.shape[1]
    tap_count = conv_weights.shape[1]
    seq_count = lax.axis_size("seq")
    seq_index = lax.axis_index("seq")
    tails_local = hyena_qkv[:, tok_local - (tap_count - 1) :, :]
    tails_prev = shifted(tails_local, "seq", 1)
    extended = jnp.concatenate([tails_prev, hyena_qkv], axis=1)
    q_feat, k_feat, v_feat = short_features(extended, conv_weights, tok_local)
    product_in = k_feat * v_feat
    sub_len = 16
    inner, starts, local_end = modal_local(product_in, decay_rates, residues, sub_len)
    piece = lax.all_gather(local_end[None], "seq", axis=0, tiled=True)
    count = piece.shape[0]
    sources = jnp.arange(count, dtype=jnp.int32)
    gap_len = jnp.maximum(seq_index - 1 - sources, 0).astype(jnp.float32) * tok_local
    factors = jnp.where(
        (sources < seq_index)[:, None, None],
        jnp.exp(-decay_rates[None, :, :] * gap_len[:, None, None]),
        0.0,
    )
    folded = jnp.sum(factors * piece, axis=0)
    incoming = (
        folded + jnp.exp(-decay_rates * (seq_index.astype(jnp.float32) * tok_local)) * prior_state
    )
    filtered = modal_readout(inner, starts, incoming, decay_rates, residues, sub_len)
    vocab_ids = jnp.arange(embed_table.shape[0], dtype=jnp.int32)
    one_hot = (token_ids[:, None] == vocab_ids[None, :]).astype(jnp.bfloat16)
    embedded = jnp.dot(one_hot, embed_table, preferred_element_type=jnp.float32)
    hyena_out = (embedded + q_feat * filtered).astype(jnp.bfloat16)
    lag_after = (seq_count - 1 - seq_index).astype(jnp.float32) * tok_local
    end_term = jnp.exp(-decay_rates * lag_after) * local_end
    end_share = lax.psum_scatter(end_term, "seq", scatter_dimension=1, tiled=True)
    share_cols = end_share.shape[1]
    rate_share = lax.dynamic_slice_in_dim(decay_rates, seq_index * share_cols, share_cols, 1)
    prior_share = lax.dynamic_slice_in_dim(prior_state, seq_index * share_cols, share_cols, 1)
    end_state = end_share + jnp.exp(-rate_share * float(seq_count * tok_local)) * prior_share
    return (hyena_out, end_state)


def solution(mesh):
    return jax.shard_map(
        body,
        mesh=mesh,
        in_specs=(
            P(("groups", "seq")),
            P(None, "tp"),
            P(None, ("groups", "seq"), "tp"),
            P(None, None, "tp"),
            P(None, "tp"),
            P(None, "tp"),
            P("groups", "tp"),
        ),
        out_specs=(P(("groups", "seq"), "tp"), P("groups", ("tp", "seq"))),
        check_vma=False,
    )
```

profile of v0, /device:TPU:0, one launch (start us, length us, event | category | flops | bytes accessed | tf_op | source)
XLA Modules:
  0.0 314.5 jit_solution(10934826178639866437)
XLA Ops:
  7.2 1.1 slice.105
  8.3 4.9 %collective-permute-start = (bf16[3,2,2048]{2,1,0:T(2,128)(2,1)S(1)}, bf16[3,2,2048]{2,1,0:T(2,128)(2,1)S(1)}, u32[]{:S(2)}, u32[]{:S(2)}) collective-permute-start(bf16[3,2,2048]{2,1,0:T(2,128)(2,1)S(1)} %slice.105), channel_id=1, source_target_pairs={{0,2},{2,4},{4,6},{6,8},{8,10},{10,12},{12,14},{1,3},{3,5},{5,7},{... | collective-permute-start | bytes 73736 | tf_op jit(solution)/shard_map/ppermute | solution.py:10
  14.3 1.6 fusion.36
  15.9 0.9 fusion.37
  17.2 1.4 copy.128
  18.5 2.1 copy.127
  20.7 2.6 fusion.31
  23.3 1.6 fusion.19
  24.9 6.0 %copy.126 = f32[8,16,2048]{1,0,2:T(8,128)} copy(f32[8,16,2048]{2,1,0:T(8,128)} %fusion.19) | data formatting | bytes 2097152 | tf_op jit(solution)/shard_map/mul | solution.py:78
  30.9 22.8 %fusion.14 = f32[8,8,2048]{0,1,2:T(8,128)} fusion(f32[8,16,2048]{1,0,2:T(8,128)} %copy.126, f32[16]{0:T(128)S(1)} %iota_subtract_fusion, f32[8,2048]{0,1:T(8,128)} %copy.128, f32[8,2048]{0,1:T(8,128)S(1)} %copy.110), kind=kOutput, calls=%fused_computation.23 | convolution fusion | flops 25690112 | bytes 1704000 | tf_op jit(solution)/shard_map/bsc,msc->bmc/dot_general | solution.py:45
  53.6 5.9 %copy.130 = f32[8,8,2048]{2,1,0:T(8,128)} copy(f32[8,8,2048]{0,1,2:T(8,128)} %fusion.14) | data formatting | bytes 1048576
  59.6 12.2 %while.14 = (s32[]{:T(128)}, f32[8,2048]{1,0:T(8,128)S(1)}, f32[8,8,2048]{2,1,0:T(8,128)}, f32[8,2048]{1,0:T(8,128)S(1)}, f32[8,8,2048]{2,1,0:T(8,128)}) while((s32[]{:T(128)}, f32[8,2048]{1,0:T(8,128)S(1)}, f32[8,8,2048]{2,1,0:T(8,128)}, f32[8,2048]{1,0:T(8,128)S(1)}, f32[8,8,2048]{2,1,0:T(8,128)}) %tuple.65), condition=%wide.region_2.3_spmd.clone.clone, body=%wide.region_1.2_spmd.clone.sunk.clone | while | flops 65539 | bytes 393804 | solution.py:51
  60.2 0.9 bitcast_add_fusion.4
  61.7 0.9 bitcast_add_fusion.4
  63.3 0.9 bitcast_add_fusion.4
  64.8 0.9 bitcast_add_fusion.4
  70.9 0.9 bitcast_add_fusion.4
  71.8 32.0 %all-gather = f32[64,2048]{1,0:T(8,128)S(1)} all-gather(f32[8,2048]{1,0:T(8,128)S(1)} %get-tuple-element.31), channel_id=2, replica_groups=mesh['groups'=2,'seq'=8,'tp'=2] {'seq'}, dimensions={0}, use_global_device_ids=true | all-gather | bytes 589824 | tf_op jit(solution)/shard_map/all_gather | solution.py:81
  104.1 1.5 exponential_multiply_fusion
  105.6 1.3 copy.109
  107.0 15.3 %multiply_reduce_fusion = f32[16,2048]{0,1:T(8,128)} fusion(f32[8,2048]{0,1:T(8,128)S(1)} %copy.110, f32[8,2048]{0,1:T(8,128)} %copy.109), kind=kLoop, calls=%fused_computation.11 | loop fusion | flops 753664 | bytes 262144 | tf_op jit(solution)/shard_map/reduce_sum | solution.py:34
  122.2 7.5 %rev.3 = f32[16,2048]{0,1:T(8,128)S(1)} reverse(f32[16,2048]{0,1:T(8,128)} %multiply_reduce_fusion), dimensions={0} | reverse | bytes 262144 | tf_op jit(solution)/shard_map/rev | solution.py:36
  129.7 7.5 %pad_slice_fusion.10 = (f32[16,2048]{0,1:T(8,128)}, f32[16,2048]{0,1:T(8,128)}, f32[16,2048]{0,1:T(8,128)}, f32[16,2048]{0,1:T(8,128)}, f32[16,2048]{0,1:T(8,128...) fusion(f32[16,2048]{0,1:T(8,128)S(1)} %rev.3), kind=kLoop, calls=%fused_computation.60 | loop fusion | bytes 2097152 | tf_op jit(solution)/shard_map/slice | solution.py:39
  137.2 1.0 multiply_add_fusion
  138.2 5.8 %copy.131 = f32[8,8,2048]{1,0,2:T(8,128)} copy(f32[8,8,2048]{2,1,0:T(8,128)} %multiply_add_fusion) | data formatting | bytes 1048576 | tf_op jit(solution)/shard_map/add | solution.py:59
  144.0 19.9 %fusion.4 = f32[2048,16,8]{1,2,0:T(8,128)} fusion(f32[8,8,2048]{1,0,2:T(8,128)} %copy.131, f32[16]{0:T(128)S(1)} %copy-done.10, f32[8,2048]{0,1:T(8,128)} %copy.127, f32[8,2048]{0,1:T(8,128)} %copy-done.1), kind=kOutput, calls=%fused_computation.7 | convolution fusion | flops 25690112 | bytes 1704000 | tf_op jit(solution)/shard_map/bmc,mtc->btc/dot_general | solution.py:65
  164.0 45.5 %stack.67 = f32[16,16,2048]{1,0,2:T(8,128)} concatenate(f32[1,16,2048]{1,0,2:T(1,128)} %bitcast.121, f32[1,16,2048]{1,0,2:T(1,128)} %bitcast.108, f32[1,16,2048]{1,0,2:T(1,128)} %bitcast.109, f32[1,16,2048]{1,0,2:T(1,128)} %bitcast.110, f32[1,16,2048]{1,0,2:T(1,128)} %bitcast.111, f32[1,16,2048]{1,0,2:T(1,128)} %bitcast.112, f32[1,16,2048]{1,0,2:T(1,128)} %bitcast.113, ...), dimensions={0} | concatenate | bytes 4194304 | tf_op jit(solution)/shard_map/stack | solution.py:38
  209.5 31.7 %bitcast_add_fusion.1 = f32[8,16,2048]{1,0,2:T(8,128)} fusion(f32[2048,16,8]{1,2,0:T(8,128)} %fusion.4, f32[8,16,2048]{1,0,2:T(8,128)} %copy.126, f32[16,16,2048]{1,0,2:T(8,128)} %stack.67), kind=kOutput, calls=%fused_computation.2 | convolution fusion | flops 50593792 | bytes 5242880 | tf_op jit(solution)/shard_map/tsc,bsc->btc/dot_general | solution.py:41
  241.2 5.1 %copy.132 = f32[8,16,2048]{2,1,0:T(8,128)S(1)} copy(f32[8,16,2048]{1,0,2:T(8,128)} %bitcast_add_fusion.1) | data formatting | bytes 2097152 | tf_op jit(solution)/shard_map/add | solution.py:66
  246.4 3.3 %fusion.17 = bf16[128,2048]{1,0:T(8,128)(2,1)} fusion(bf16[512,2048]{1,0:T(8,128)(2,1)S(1)} %copy-done, f32[128,2048]{1,0:T(8,128)S(1)} %bitcast.128, bf16[3,128,2048]{2,1,0:T(8,128)(2,1)} %param.11, bf16[3,2,2048]{2,1,0:T(2,128)(2,1)S(1)} %copy-done.6, f32[2048]{0:T(1024)S(1)} %bitcast.136, f32[2048]{0:T(1024)S(1)} %bitcast.137, f32[2048]{0:T(1024)S(1)} %bitcast.135, ...), kind=kOutput, calls=%fused_computation.25 | convolution fusion | flops 273481728 | bytes 5816832 | tf_op jit(solution)/shard_map/dot_general | solution.py:97
  249.7 56.6 %reduce-scatter.2.cloned.1.call-done = f32[8,256]{1,0:T(8,128)} async-done(((f32[8,2048]{1,0:T(8,128)}), f32[8,256]{1,0:T(8,128)}) %reduce-scatter.2.cloned.1.call-update) | async-done | bytes 8208 | tf_op jit(solution)/shard_map/reduce_scatter | solution.py:101
  306.3 1.3 multiply_add_fusion.2
  (45 shorter events, 9.5 us)
Async XLA Ops:
  7.2 239.2 %copy-start = (bf16[512,2048]{1,0:T(8,128)(2,1)S(1)}, bf16[512,2048]{1,0:T(8,128)(2,1)}, u32[]{:S(2)}) copy-start(bf16[512,2048]{1,0:T(8,128)(2,1)} %param.10) | copy-start | bytes 6291460
  7.2 299.2 %reduce-scatter.2.cloned.1.call-start = ((), (), s32[]{:S(2)}) async-start(), calls=%async_computation.1 | async-start | bytes 73728 | tf_op jit(solution)/shard_map/reduce_scatter | solution.py:101
  8.3 12.4 %collective-permute-start = (bf16[3,2,2048]{2,1,0:T(2,128)(2,1)S(1)}, bf16[3,2,2048]{2,1,0:T(2,128)(2,1)S(1)}, u32[]{:S(2)}, u32[]{:S(2)}) collective-permute-start(bf16[3,2,2048]{2,1,0:T(2,128)(2,1)S(1)} %slice.105), channel_id=1, source_target_pairs={{0,2},{2,4},{4,6},{6,8},{8,10},{10,12},{12,14},{1,3},{3,5},{5,7},{... | collective-permute-start | bytes 73736 | tf_op jit(solution)/shard_map/ppermute | solution.py:10
  17.2 89.8 %copy-start.1 = (f32[8,2048]{0,1:T(8,128)}, f32[8,2048]{0,1:T(8,128)S(1)}, u32[]{:S(2)}) copy-start(f32[8,2048]{0,1:T(8,128)S(1)} %copy.110) | copy-start | bytes 196612
  20.7 10.2 %copy-start.5 = (bf16[3,2,2048]{2,1,0:T(2,128)(2,1)}, bf16[3,2,2048]{2,1,0:T(2,128)(2,1)S(1)}, u32[]{:S(2)}) copy-start(bf16[3,2,2048]{2,1,0:T(2,128)(2,1)S(1)} %collective-permute-done) | copy-start | bytes 73732
  53.6 50.4 %copy-start.3 = (f32[8,2048]{1,0:T(8,128)S(1)}, f32[8,2048]{1,0:T(8,128)}, u32[]{:S(2)}) copy-start(f32[8,2048]{1,0:T(8,128)} %param.13) | copy-start | bytes 196612
  53.6 50.4 %copy-start.4 = (f32[8,2048]{1,0:T(8,128)S(1)}, f32[8,2048]{1,0:T(8,128)}, u32[]{:S(2)}) copy-start(f32[8,2048]{1,0:T(8,128)} %param.14) | copy-start | bytes 196612
  129.7 7.5 %copy-start.2 = (f32[8,8,2048]{2,1,0:T(8,128)S(1)}, f32[8,8,2048]{2,1,0:T(8,128)}, u32[]{:S(2)}) copy-start(f32[8,8,2048]{2,1,0:T(8,128)} %get-tuple-element.30) | copy-start | bytes 1572868
  129.7 7.5 %copy-start.8 = (f32[8]{0:T(128)S(1)}, f32[8]{0:T(128)}, u32[]{:S(2)}) copy-start(f32[8]{0:T(128)} %iota_multiply_fusion) | copy-start | bytes 100
  137.2 6.8 %copy-start.10 = (f32[16]{0:T(128)S(1)}, f32[16]{0:T(128)}, u32[]{:S(2)}) copy-start(f32[16]{0:T(128)} %iota_add_fusion) | copy-start | bytes 196
  241.2 5.2 %copy-start.6 = (bf16[3,2,2048]{2,1,0:T(2,128)(2,1)S(1)}, bf16[3,2,2048]{2,1,0:T(2,128)(2,1)}, u32[]{:S(2)}) copy-start(bf16[3,2,2048]{2,1,0:T(2,128)(2,1)} %copy-done.5) | copy-start | bytes 73732
  241.2 5.2 %copy-start.7 = (f32[1,1,2048]{2,1,0:T(1,128)S(1)}, f32[1,1,2048]{2,1,0:T(1,128)}, u32[]{:S(2)}) copy-start(f32[1,1,2048]{2,1,0:T(1,128)} %get-tuple-element.112) | copy-start | bytes 24580
  241.2 5.2 %copy-start.9 = (s32[128]{0:T(128)S(1)}, s32[128]{0:T(128)}, u32[]{:S(2)}) copy-start(s32[128]{0:T(128)} %param.9) | copy-start | bytes 1540
Sparse Core Ops, SparseCore 0:
  246.5 59.7 reduce-scatter.1
where the time goes:
time: 321 us; the launch traced here: 315 us
  local copies, waits for them, and re-layouts  91.3 us (28%)
  matrix products  77.7 us (24%)
  waiting for transfers between devices  56.6 us (18%)
  other arithmetic  37.6 us (12%)
  blocking collectives  32 us (10%)
  between operations  14.2 us (4%)
  starting transfers between devices  4.91 us (2%)
    reduce_scatter x1, waiting for transfers between devices, body(): lax.psum_scatter(end_term, 'seq', scatter_dimension=1, tiled=True)  56.6 us
    another operation x1, local copies, waits for them, and re-layouts, modal_local(): jnp.stack([extended[sub_len - 1 - row:2 * sub_len - 1 - row] for row in r...  45.5 us
    all_gather x1, blocking collectives, body(): piece = lax.all_gather(local_end[None], 'seq', axis=0, tiled=True)  32 us
    dot_general x1, matrix products, modal_local(): jnp.einsum('tsc,bsc->btc', toeplitz, blocks, precision=lax.Precision.HIGH...  31.7 us
    dot_general x1, matrix products, modal_local(): jnp.einsum('bsc,msc->bmc', blocks, tail_weight, precision=lax.Precision.H...  22.8 us
    dot_general x1, matrix products, modal_readout(): jnp.einsum('bmc,mtc->btc', opening, readout, precision=lax.Precision.HIGH...  19.9 us
    reduce_sum x1, other arithmetic, modal_local(): kernel = jnp.sum((residues * gain)[:, None, :] * decay_table, axis=0)  15.3 us
    unnamed x24, local copies, waits for them, and re-layouts  8.12 us
  transfers between devices with their start and end apart: 2, of which 1 were waited for; matrix products, arithmetic and copies ran while one was open for 3% of the time, Pallas kernels for 0%

commit v1 on v0

--- a/solution.py
+++ b/solution.py
@@ -1,6 +1,9 @@
+import functools
 import jax
 import jax.numpy as jnp
 from jax import lax
+from jax.experimental import pallas as pl
+from jax.experimental.pallas import tpu as pltpu
 from jax.sharding import PartitionSpec as P
 
 
@@ -66,7 +69,7 @@
     return (inner + outer).reshape(block_count * sub_len, inner.shape[2])
 
 
-def body(token_ids, embed_table, hyena_qkv, conv_weights, decay_rates, residues, prior_state):
+def plain_body(token_ids, embed_table, hyena_qkv, conv_weights, decay_rates, residues, prior_state):
     tok_local = hyena_qkv.shape[1]
     tap_count = conv_weights.shape[1]
     seq_count = lax.axis_size("seq")
@@ -106,6 +109,357 @@
     return (hyena_out, end_state)
 
 
+LANES = 128
+SUBL = 8
+MESH = pl.DeviceIdType.MESH
+
+
+def one_minus_exp(y):
+    series = jnp.ones_like(y)
+    for k in range(9, 1, -1):
+        series = 1.0 - (y / k) * series
+    return jnp.where(y < 0.5, y * series, 1.0 - jnp.exp(-y))
+
+
+def fused_kernel(
+    n, ids_ref, emb_hbm, qkv_hbm, cw_hbm, rate_hbm, res_hbm, prior_hbm,
+    out_hbm, end_ref,
+    qkv_v, emb_v, cw_v, rate_v, res_v, prior_v, out_v,
+    tail32, tail_send, tail_recv, ext, q_s, p_s, f_s, g_s,
+    rate_r, pole_r, gain_r, rg_r, res_r, prior_r, ends, gath, pref, inc,
+    load_sem, tail_sem, s1_sem, r1_sem, s2_sem, r2_sem, out_sem,
+):
+    members, tok, chans = qkv_v.shape
+    blocks = chans // LANES
+    halves = blocks // SUBL
+    pitch = tok + SUBL
+    modes = SUBL
+    rows = blocks // n * modes
+    half_cols = SUBL * LANES
+    me = lax.axis_index("seq")
+
+    loads = [
+        pltpu.make_async_copy(src, dst, load_sem.at[i])
+        for i, (src, dst) in enumerate(
+            (
+                (qkv_hbm, qkv_v),
+                (rate_hbm, rate_v),
+                (res_hbm, res_v),
+                (prior_hbm, prior_v),
+                (cw_hbm, cw_v),
+                (emb_hbm, emb_v),
+            )
+        )
+    ]
+    for load in loads:
+        load.start()
+
+    barrier = pltpu.get_barrier_semaphore()
+    for d in range(1, n):
+        pl.semaphore_signal(
+            barrier, inc=1, device_id={"seq": lax.rem(me + d, n)}, device_id_type=MESH
+        )
+
+    loads[0].wait()
+
+    def pack_tail(b, _):
+        cols = pl.ds(pl.multiple_of(b * LANES, LANES), LANES)
+        for m in range(members):
+            last = qkv_v[m, tok - 16 : tok, cols].astype(jnp.float32)
+            tail32[pl.ds((m * blocks + b) * 2, 2), :] = last[14:16]
+        return 0
+
+    lax.fori_loop(0, blocks, pack_tail, 0, unroll=4)
+    tail_send[...] = tail32[...].astype(jnp.bfloat16)
+    pl.semaphore_wait(barrier, n - 1)
+    tail_copy = pltpu.make_async_remote_copy(
+        src_ref=tail_send,
+        dst_ref=tail_recv,
+        send_sem=tail_sem.at[0],
+        recv_sem=tail_sem.at[1],
+        device_id={"seq": lax.rem(me + 1, n)},
+        device_id_type=MESH,
+    )
+    tail_copy.start()
+
+    for load in loads[1:5]:
+        load.wait()
+    rate = rate_v[...]
+    pole = jnp.exp(-rate)
+    gain = jnp.sqrt(one_minus_exp(2.0 * rate))
+    res = res_v[...]
+    prior = prior_v[...]
+    for b in range(blocks):
+        cut = slice(b * LANES, (b + 1) * LANES)
+        put = slice(b * modes, (b + 1) * modes)
+        rate_r[put, :] = rate[:, cut]
+        pole_r[put, :] = pole[:, cut]
+        gain_r[put, :] = gain[:, cut]
+        rg_r[put, :] = (res * gain)[:, cut]
+        res_r[put, :] = res[:, cut]
+        prior_r[put, :] = prior[:, cut]
+
+    for m in range(members):
+        ext[m, 0:SUBL, :] = jnp.zeros((SUBL, LANES), jnp.float32)
+
+    def taps(m, cols):
+        return [cw_v[m, j : j + 1, cols] for j in range(3)]
+
+    def short(b, _):
+        cols = pl.ds(pl.multiple_of(b * LANES, LANES), LANES)
+        feats = []
+        for m in range(members):
+            w0, w1, w2 = taps(m, cols)
+            now = qkv_v[m, :, cols].astype(jnp.float32)
+            ext[m, SUBL:, :] = now
+            feats.append(
+                w0 * now
+                + w1 * ext[m, SUBL - 1 : SUBL - 1 + tok, :]
+                + w2 * ext[m, SUBL - 2 : SUBL - 2 + tok, :]
+            )
+        q_s[pl.ds(pl.multiple_of(b * tok, SUBL), tok), :] = feats[0]
+        p_s[pl.ds(pl.multiple_of(b * pitch, SUBL), tok), :] = feats[1] * feats[2]
+        return 0
+
+    lax.fori_loop(0, blocks, short, 0)
+
+    def per_mode(ref):
+        return [
+            ref[pl.ds(h * SUBL * modes + m, SUBL, stride=modes), :]
+            for h in range(halves)
+            for m in range(modes)
+        ]
+
+    def tokens(ref, t):
+        return [ref[pl.ds(h * SUBL * pitch + t, SUBL, stride=pitch), :] for h in range(halves)]
+
+    poles = per_mode(pole_r)
+
+    def horner(t, state):
+        now = tokens(p_s, t)
+        return tuple(poles[i] * s + now[i // modes] for i, s in enumerate(state))
+
+    zeros = tuple(jnp.zeros((SUBL, LANES), jnp.float32) for _ in range(halves * modes))
+    late = lax.fori_loop(2, tok, horner, zeros, unroll=6)
+
+    for i, s in enumerate(late):
+        h, m = divmod(i, modes)
+        ends[pl.ds(h * SUBL * modes + m, SUBL, stride=modes), :] = s
+    tail_copy.wait_recv()
+    tail32[...] = jnp.where(me > 0, tail_recv[...].astype(jnp.float32), 0.0)
+
+    def patch(b, _):
+        cols = pl.ds(pl.multiple_of(b * LANES, LANES), LANES)
+        feats = []
+        for m in range(members):
+            w0, w1, w2 = taps(m, cols)
+            now = qkv_v[m, 0:16, cols].astype(jnp.float32)[0:SUBL]
+            ext[m, SUBL - 2 : SUBL, :] = tail32[pl.ds((m * blocks + b) * 2, 2), :]
+            ext[m, SUBL : 2 * SUBL, :] = now
+            feats.append(
+                w0 * now
+                + w1 * ext[m, SUBL - 1 : 2 * SUBL - 1, :]
+                + w2 * ext[m, SUBL - 2 : 2 * SUBL - 2, :]
+            )
+        q_s[pl.ds(pl.multiple_of(b * tok, SUBL), SUBL), :] = feats[0]
+        p_s[pl.ds(pl.multiple_of(b * pitch, SUBL), SUBL), :] = feats[1] * feats[2]
+        return 0
+
+    lax.fori_loop(0, blocks, patch, 0, unroll=2)
+    first, second = tokens(p_s, 0), tokens(p_s, 1)
+    lag = jnp.exp(-rate_r[...] * float(tok - 2))
+    pref[0 : blocks * modes, :] = lag
+    lags = per_mode(pref)
+    gains = per_mode(gain_r)
+    olds = per_mode(ends)
+    for i in range(halves * modes):
+        h, m = divmod(i, modes)
+        early = poles[i] * first[h] + second[h]
+        ends[pl.ds(h * SUBL * modes + m, SUBL, stride=modes), :] = gains[i] * (
+            lags[i] * early + olds[i]
+        )
+
+    def chunk(index):
+        return pl.ds(pl.multiple_of(index * rows, SUBL), rows)
+
+    sends = []
+    for d in range(1, n):
+        peer = lax.rem(me + d, n)
+        copy = pltpu.make_async_remote_copy(
+            src_ref=ends.at[chunk(peer)],
+            dst_ref=gath.at[chunk(me)],
+            send_sem=s1_sem.at[d],
+            recv_sem=r1_sem.at[d],
+            device_id={"seq": peer},
+            device_id_type=MESH,
+        )
+        copy.start()
+        sends.append(copy)
+    gath[chunk(me), :] = ends[chunk(me), :]
+
+    weights = per_mode(rg_r)
+
+    def scan(t, state):
+        now = tokens(p_s, t)
+        state = tuple(poles[i] * s + now[i // modes] for i, s in enumerate(state))
+        for h in range(halves):
+            terms = [weights[i] * state[i] for i in range(h * modes, (h + 1) * modes)]
+            while len(terms) > 1:
+                terms = [a + b for a, b in zip(terms[::2], terms[1::2])]
+            f_s[pl.ds(h * SUBL * pitch + t, SUBL, stride=pitch), :] = terms[0]
+        return state
+
+    lax.fori_loop(0, tok, scan, zeros, unroll=4)
+
+    for copy in sends:
+        copy.wait_recv()
+    step = jnp.exp(-rate_r[chunk(me), :] * float(tok))
+    state = prior_r[chunk(me), :]
+    for copy in sends:
+        copy.wait_send()
+    for i in range(n):
+        pref[i * rows : (i + 1) * rows, :] = state
+        state = step * state + gath[i * rows : (i + 1) * rows, :]
+
+    returns = []
+    for d in range(1, n):
+        peer = lax.rem(me + d, n)
+        copy = pltpu.make_async_remote_copy(
+            src_ref=pref.at[chunk(peer)],
+            dst_ref=inc.at[chunk(me)],
+            send_sem=s2_sem.at[d],
+            recv_sem=r2_sem.at[d],
+            device_id={"seq": peer},
+            device_id_type=MESH,
+        )
+        copy.start()
+        returns.append(copy)
+    inc[chunk(me), :] = pref[chunk(me), :]
+    for b in range(rows // modes):
+        end_ref[:, b * LANES : (b + 1) * LANES] = state[b * modes : (b + 1) * modes]
+
+    loads[5].wait()
+    vocab = emb_v.shape[0]
+    which = lax.broadcasted_iota(jnp.int32, (vocab, tok), 0) == ids_ref[...]
+    one_hot = jnp.where(which, 1.0, 0.0).astype(jnp.bfloat16)
+    wide = 2 * LANES
+
+    def embed(b, _):
+        cols = pl.ds(pl.multiple_of(b * wide, wide), wide)
+        g_s[:, cols] = lax.dot_general(
+            one_hot, emb_v[:, cols], (((0,), (0,)), ((), ())),
+            preferred_element_type=jnp.float32,
+        )
+        return 0
+
+    lax.fori_loop(0, chans // wide, embed, 0)
+
+    for copy in returns:
+        copy.wait_recv()
+    inc[...] = res_r[...] * inc[...]
+    shares = per_mode(inc)
+    stores = []
+    for h in range(halves):
+        half_poles = poles[h * modes : (h + 1) * modes]
+
+        def carried(t, share, h=h, half_poles=half_poles):
+            share = tuple(p * s for p, s in zip(half_poles, share))
+            terms = list(share)
+            while len(terms) > 1:
+                terms = [a + b for a, b in zip(terms[::2], terms[1::2])]
+            spot = pl.ds(h * SUBL * pitch + t, SUBL, stride=pitch)
+            f_s[spot, :] = f_s[spot, :] + terms[0]
+            return share
+
+        lax.fori_loop(
+            0, tok, carried, tuple(shares[h * modes : (h + 1) * modes]), unroll=8
+        )
+
+        def finish(b, _):
+            cols = pl.ds(pl.multiple_of(b * LANES, LANES), LANES)
+            filtered = f_s[pl.ds(pl.multiple_of(b * pitch, SUBL), tok), :]
+            q_feat = q_s[pl.ds(pl.multiple_of(b * tok, SUBL), tok), :]
+            out_v[:, cols] = (g_s[:, cols] + q_feat * filtered).astype(jnp.bfloat16)
+            return 0
+
+        lax.fori_loop(h * SUBL, (h + 1) * SUBL, finish, 0)
+        span = pl.ds(h * half_cols, half_cols)
+        store = pltpu.make_async_copy(out_v.at[:, span], out_hbm.at[:, span], out_sem.at[h])
+        store.start()
+        stores.append(store)
+    tail_copy.wait_send()
+    for copy in returns:
+        copy.wait_send()
+    for store in stores:
+        store.wait()
+
+
+def fused_body(token_ids, embed_table, hyena_qkv, conv_weights, decay_rates, residues, prior_state):
+    n = lax.axis_size("seq")
+    members, tok, chans = hyena_qkv.shape
+    modes = decay_rates.shape[0]
+    blocks = chans // LANES
+    table = pltpu.VMEM((blocks * modes, LANES), jnp.float32)
+    f32 = jnp.float32
+    padded = blocks * (tok + SUBL)
+    scratch = [
+        pltpu.VMEM(hyena_qkv.shape, jnp.bfloat16),
+        pltpu.VMEM(embed_table.shape, jnp.bfloat16),
+        pltpu.VMEM(conv_weights.shape, f32),
+        pltpu.VMEM(decay_rates.shape, f32),
+        pltpu.VMEM(residues.shape, f32),
+        pltpu.VMEM(prior_state.shape, f32),
+        pltpu.VMEM((tok, chans), jnp.bfloat16),
+        pltpu.VMEM((members * blocks * 2, LANES), f32),
+        pltpu.VMEM((members * blocks * 2, LANES), jnp.bfloat16),
+        pltpu.VMEM((members * blocks * 2, LANES), jnp.bfloat16),
+        pltpu.VMEM((members, tok + SUBL, LANES), f32),
+        pltpu.VMEM((blocks * tok, LANES), f32),
+        pltpu.VMEM((padded, LANES), f32),
+        pltpu.VMEM((padded, LANES), f32),
+        pltpu.VMEM((tok, chans), f32),
+    ] + [table] * 10 + [
+        pltpu.SemaphoreType.DMA((6,)),
+        pltpu.SemaphoreType.DMA((2,)),
+    ] + [pltpu.SemaphoreType.DMA((n,))] * 4 + [
+        pltpu.SemaphoreType.DMA((blocks // SUBL,)),
+    ]
+    any_spec = pl.BlockSpec(memory_space=pl.ANY)
+    vmem_spec = pl.BlockSpec(memory_space=pltpu.VMEM)
+    return pl.pallas_call(
+        functools.partial(fused_kernel, n),
+        out_shape=(
+            jax.ShapeDtypeStruct((tok, chans), jnp.bfloat16),
+            jax.ShapeDtypeStruct((modes, chans // n), f32),
+        ),
+        in_specs=[vmem_spec] + [any_spec] * 6,
+        out_specs=(any_spec, vmem_spec),
+        scratch_shapes=scratch,
+        compiler_params=pltpu.CompilerParams(
+            collective_id=0, has_side_effects=True, vmem_limit_bytes=40 * 1024 * 1024
+        ),
+    )(
+        token_ids.reshape(1, tok), embed_table, hyena_qkv, conv_weights,
+        decay_rates, residues, prior_state,
+    )
+
+
+def body(token_ids, embed_table, hyena_qkv, conv_weights, decay_rates, residues, prior_state):
+    n = lax.axis_size("seq")
+    members, tok, chans = hyena_qkv.shape
+    fits = (
+        chans % (n * LANES) == 0
+        and chans % (SUBL * LANES) == 0
+        and tok % LANES == 0
+        and decay_rates.shape[0] == SUBL
+        and conv_weights.shape[1] == 3
+    )
+    run = fused_body if fits else plain_body
+    return run(
+        token_ids, embed_table, hyena_qkv, conv_weights, decay_rates, residues, prior_state
+    )
+
+
 def solution(mesh):
     return jax.shard_map(
         body,

time: 321 us -> 29.3 us (0.09); the launches traced: 315 us -> 29 us
  local copies, waits for them, and re-layouts: 91.3 us -> 8.45 us
  matrix products: 77.7 us -> 0 us
  waiting for transfers between devices: 56.6 us -> 0 us
  other arithmetic: 37.6 us -> 0 us
  blocking collectives: 32 us -> 0 us
  Pallas kernels: 0 us -> 19.9 us
  between operations: 14.2 us -> 0.66 us
  starting transfers between devices: 4.91 us -> 0 us
    dot_general x4 -> x0, matrix products: 77.7 us -> none  [the longest x1 31.7 us: modal_local(): jnp.einsum('tsc,bsc->btc', toeplitz, blocks, precision=lax.Precision.HIGH...]
    reduce_scatter x1 -> x0, waiting for transfers between devices: 56.6 us -> none  [body(): lax.psum_scatter(end_term, 'seq', scatter_dimension=1, tiled=True)]
    another operation x1 -> x0, local copies, waits for them, and re-layouts: 45.5 us -> none  [modal_local(): jnp.stack([extended[sub_len - 1 - row:2 * sub_len - 1 - row] for row in r...]
    all_gather x1 -> x0, blocking collectives: 32 us -> none  [body(): piece = lax.all_gather(local_end[None], 'seq', axis=0, tiled=True)]
    pallas_call x0 -> x1, Pallas kernels: none -> 19.9 us  [fused_body(): pl.pallas_call(functools.partial(fused_kernel, n), out_shape=(jax.ShapeDt...]
    reduce_sum x2 -> x0, other arithmetic: 15.4 us -> none  [the longest x1 15.3 us: modal_local(): kernel = jnp.sum((residues * gain)[:, None, :] * decay_table, axis=0)]
    add x2 -> x0, local copies, waits for them, and re-layouts: 11 us -> none  [the longest x1 5.85 us: modal_readout(): starts + jnp.exp(-decay_rates[None, :, :] * block_pos[:, None, None]) * i...]
    slice x3 -> x0, local copies, waits for them, and re-layouts: 10.2 us -> none  [the longest x1 7.5 us: modal_local(): extended[sub_len - 1 - row:2 * sub_len - 1 - row]]
  transfers between devices with their start and end apart: 2 -> 0, of which waited for: 1 -> 0; matrix products, arithmetic and copies ran while one was open for 3% -> 0% of each run, Pallas kernels for 0% -> 0%
where the time goes in v1:
time: 29.3 us; the launch traced here: 29 us
  Pallas kernels  19.9 us (68%)
  local copies, waits for them, and re-layouts  8.45 us (29%)
  between operations  0.66 us (2%)
    pallas_call x1, Pallas kernels, fused_body(): pl.pallas_call(functools.partial(fused_kernel, n), out_shape=(jax.ShapeDt...  19.9 us
    unnamed x16, local copies, waits for them, and re-layouts  8.45 us

profile of v1, /device:TPU:0, one launch (start us, length us, event | category | flops | bytes accessed | tf_op | source)
XLA Modules:
  0.0 29.0 jit_solution(11200145376169900499)
XLA Ops:
  0.6 0.0 copy-start
  0.6 1.6 %copy-done = bf16[512,2048]{1,0:T(8,128)(2,1)S(1)} copy-done((bf16[512,2048]{1,0:T(8,128)(2,1)S(1)}, bf16[512,2048]{1,0:T(8,128)(2,1)}, u32[]{:S(2)}) %copy-start) | copy-done | bytes 2097176
  2.2 0.0 copy-start.1
  2.2 1.4 %copy-done.1 = bf16[3,128,2048]{2,1,0:T(8,128)(2,1)S(1)} copy-done((bf16[3,128,2048]{2,1,0:T(8,128)(2,1)S(1)}, bf16[3,128,2048]{2,1,0:T(8,128)(2,1)}, u32[]{:S(2)}) %copy-start.1) | copy-done | bytes 1572888
  3.6 0.0 copy-start.2
  3.6 0.9 %copy-done.2 = f32[3,3,2048]{2,1,0:T(4,128)S(1)} copy-done((f32[3,3,2048]{2,1,0:T(4,128)S(1)}, f32[3,3,2048]{2,1,0:T(4,128)}, u32[]{:S(2)}) %copy-start.2) | copy-done | bytes 73752
  4.5 0.0 copy-start.3
  4.5 0.8 %copy-done.3 = f32[8,2048]{1,0:T(8,128)S(1)} copy-done((f32[8,2048]{1,0:T(8,128)S(1)}, f32[8,2048]{1,0:T(8,128)}, u32[]{:S(2)}) %copy-start.3) | copy-done | bytes 65560
  5.4 0.0 copy-start.4
  5.4 0.8 %copy-done.4 = f32[8,2048]{1,0:T(8,128)S(1)} copy-done((f32[8,2048]{1,0:T(8,128)S(1)}, f32[8,2048]{1,0:T(8,128)}, u32[]{:S(2)}) %copy-start.4) | copy-done | bytes 65560
  6.2 0.0 copy-start.5
  6.2 0.8 %copy-done.5 = f32[8,2048]{1,0:T(8,128)S(1)} copy-done((f32[8,2048]{1,0:T(8,128)S(1)}, f32[8,2048]{1,0:T(8,128)}, u32[]{:S(2)}) %copy-start.5) | copy-done | bytes 65560
  7.0 0.0 copy-start.6
  7.0 0.7 %copy-done.6 = s32[128]{0:T(128)S(1)} copy-done((s32[128]{0:T(128)S(1)}, s32[128]{0:T(128)}, u32[]{:S(2)}) %copy-start.6) | copy-done | bytes 536
  7.7 19.9 %shard_map.86 = (bf16[128,2048]{1,0:T(8,128)(2,1)S(1)}, f32[8,256]{1,0:T(8,128)S(1)}) custom-call(s32[1,128]{1,0:T(1,128)S(1)} %bitcast.1, bf16[512,2048]{1,0:T(8,128)(2,1)S(1)} %copy-done, bf16[3,128,2048]{2,1,0:T(8,128)(2,1)S(1)} %copy-done.1, f32[3,3,2048]{2,1,0:T(4,128)S(1)} %copy-done.2, f32[8,2048]{1,0:T(8,128)S(1)} %copy-done.3, ...), custom_call_target="tpu_custom_call" | custom-call | tf_op jit(solution)/shard_map/pallas_call | solution.py:429
  27.6 0.8 %copy.11 = bf16[128,2048]{1,0:T(8,128)(2,1)} copy(bf16[128,2048]{1,0:T(8,128)(2,1)S(1)} %get-tuple-element.4) | data formatting | bytes 1048576
  28.4 0.6 %copy.12 = f32[8,256]{1,0:T(8,128)} copy(f32[8,256]{1,0:T(8,128)S(1)} %get-tuple-element.5) | data formatting | bytes 16384
Async XLA Ops:
  0.6 1.6 %copy-start = (bf16[512,2048]{1,0:T(8,128)(2,1)S(1)}, bf16[512,2048]{1,0:T(8,128)(2,1)}, u32[]{:S(2)}) copy-start(bf16[512,2048]{1,0:T(8,128)(2,1)} %emb_hbm.1) | copy-start | bytes 6291460
  2.2 1.4 %copy-start.1 = (bf16[3,128,2048]{2,1,0:T(8,128)(2,1)S(1)}, bf16[3,128,2048]{2,1,0:T(8,128)(2,1)}, u32[]{:S(2)}) copy-start(bf16[3,128,2048]{2,1,0:T(8,128)(2,1)} %qkv_hbm.1) | copy-start | bytes 4718596
  3.6 0.9 %copy-start.2 = (f32[3,3,2048]{2,1,0:T(4,128)S(1)}, f32[3,3,2048]{2,1,0:T(4,128)}, u32[]{:S(2)}) copy-start(f32[3,3,2048]{2,1,0:T(4,128)} %cw_hbm.1) | copy-start | bytes 221188
  4.5 0.8 %copy-start.3 = (f32[8,2048]{1,0:T(8,128)S(1)}, f32[8,2048]{1,0:T(8,128)}, u32[]{:S(2)}) copy-start(f32[8,2048]{1,0:T(8,128)} %rate_hbm.1) | copy-start | bytes 196612
  5.4 0.8 %copy-start.4 = (f32[8,2048]{1,0:T(8,128)S(1)}, f32[8,2048]{1,0:T(8,128)}, u32[]{:S(2)}) copy-start(f32[8,2048]{1,0:T(8,128)} %res_hbm.1) | copy-start | bytes 196612
  6.2 0.8 %copy-start.5 = (f32[8,2048]{1,0:T(8,128)S(1)}, f32[8,2048]{1,0:T(8,128)}, u32[]{:S(2)}) copy-start(f32[8,2048]{1,0:T(8,128)} %prior_hbm.1) | copy-start | bytes 196612
  7.0 0.7 %copy-start.6 = (s32[128]{0:T(128)S(1)}, s32[128]{0:T(128)}, u32[]{:S(2)}) copy-start(s32[128]{0:T(128)} %param.7) | copy-start | bytes 1540

commit v2 on v1

--- a/solution.py
+++ b/solution.py
@@ -123,11 +123,11 @@
 
 def fused_kernel(
     n, ids_ref, emb_hbm, qkv_hbm, cw_hbm, rate_hbm, res_hbm, prior_hbm,
-    out_hbm, end_ref,
-    qkv_v, emb_v, cw_v, rate_v, res_v, prior_v, out_v,
-    tail32, tail_send, tail_recv, ext, q_s, p_s, f_s, g_s,
-    rate_r, pole_r, gain_r, rg_r, res_r, prior_r, ends, gath, pref, inc,
-    load_sem, tail_sem, s1_sem, r1_sem, s2_sem, r2_sem, out_sem,
+    inc_hbm, table_hbm, q_hbm, base_hbm, end_hbm,
+    qkv_v, emb_v, cw_v, rate_v, res_v, prior_v,
+    tail32, tail_send, tail_recv, ext, q_s, p_s, f_s, base_v, end_v, table_v,
+    rate_r, gain_r, rg_r, prior_r, ends, gath, pref,
+    load_sem, tail_sem, s1_sem, r1_sem, s2_sem, r2_sem, store_sem,
 ):
     members, tok, chans = qkv_v.shape
     blocks = chans // LANES
@@ -135,7 +135,6 @@
     pitch = tok + SUBL
     modes = SUBL
     rows = blocks // n * modes
-    half_cols = SUBL * LANES
     me = lax.axis_index("seq")
 
     loads = [
@@ -193,11 +192,13 @@
         cut = slice(b * LANES, (b + 1) * LANES)
         put = slice(b * modes, (b + 1) * modes)
         rate_r[put, :] = rate[:, cut]
-        pole_r[put, :] = pole[:, cut]
+        table_v[0, put, :] = pole[:, cut]
         gain_r[put, :] = gain[:, cut]
         rg_r[put, :] = (res * gain)[:, cut]
-        res_r[put, :] = res[:, cut]
+        table_v[1, put, :] = res[:, cut]
         prior_r[put, :] = prior[:, cut]
+    stores = [pltpu.make_async_copy(table_v, table_hbm, store_sem.at[0])]
+    stores[0].start()
 
     for m in range(members):
         ext[m, 0:SUBL, :] = jnp.zeros((SUBL, LANES), jnp.float32)
@@ -205,20 +206,20 @@
     def taps(m, cols):
         return [cw_v[m, j : j + 1, cols] for j in range(3)]
 
+    def filtered_block(m, cols):
+        w0, w1, w2 = taps(m, cols)
+        now = qkv_v[m, :, cols].astype(jnp.float32)
+        ext[m, SUBL:, :] = now
+        return (
+            w0 * now
+            + w1 * ext[m, SUBL - 1 : SUBL - 1 + tok, :]
+            + w2 * ext[m, SUBL - 2 : SUBL - 2 + tok, :]
+        )
+
     def short(b, _):
         cols = pl.ds(pl.multiple_of(b * LANES, LANES), LANES)
-        feats = []
-        for m in range(members):
-            w0, w1, w2 = taps(m, cols)
-            now = qkv_v[m, :, cols].astype(jnp.float32)
-            ext[m, SUBL:, :] = now
-            feats.append(
-                w0 * now
-                + w1 * ext[m, SUBL - 1 : SUBL - 1 + tok, :]
-                + w2 * ext[m, SUBL - 2 : SUBL - 2 + tok, :]
-            )
-        q_s[pl.ds(pl.multiple_of(b * tok, SUBL), tok), :] = feats[0]
-        p_s[pl.ds(pl.multiple_of(b * pitch, SUBL), tok), :] = feats[1] * feats[2]
+        k_feat, v_feat = [filtered_block(m, cols) for m in (1, 2)]
+        p_s[pl.ds(pl.multiple_of(b * pitch, SUBL), tok), :] = k_feat * v_feat
         return 0
 
     lax.fori_loop(0, blocks, short, 0)
@@ -233,7 +234,7 @@
     def tokens(ref, t):
         return [ref[pl.ds(h * SUBL * pitch + t, SUBL, stride=pitch), :] for h in range(halves)]
 
-    poles = per_mode(pole_r)
+    poles = per_mode(table_v.at[0])
 
     def horner(t, state):
         now = tokens(p_s, t)
@@ -251,7 +252,7 @@
     def patch(b, _):
         cols = pl.ds(pl.multiple_of(b * LANES, LANES), LANES)
         feats = []
-        for m in range(members):
+        for m in (1, 2):
             w0, w1, w2 = taps(m, cols)
             now = qkv_v[m, 0:16, cols].astype(jnp.float32)[0:SUBL]
             ext[m, SUBL - 2 : SUBL, :] = tail32[pl.ds((m * blocks + b) * 2, 2), :]
@@ -261,8 +262,7 @@
                 + w1 * ext[m, SUBL - 1 : 2 * SUBL - 1, :]
                 + w2 * ext[m, SUBL - 2 : 2 * SUBL - 2, :]
             )
-        q_s[pl.ds(pl.multiple_of(b * tok, SUBL), SUBL), :] = feats[0]
-        p_s[pl.ds(pl.multiple_of(b * pitch, SUBL), SUBL), :] = feats[1] * feats[2]
+        p_s[pl.ds(pl.multiple_of(b * pitch, SUBL), SUBL), :] = feats[0] * feats[1]
         return 0
 
     lax.fori_loop(0, blocks, patch, 0, unroll=2)
@@ -311,6 +311,16 @@
 
     lax.fori_loop(0, tok, scan, zeros, unroll=4)
 
+    def query(b, _):
+        cols = pl.ds(pl.multiple_of(b * LANES, LANES), LANES)
+        ext[0, SUBL - 2 : SUBL, :] = tail32[pl.ds(b * 2, 2), :]
+        q_s[:, cols] = filtered_block(0, cols)
+        return 0
+
+    lax.fori_loop(0, blocks, query, 0)
+    stores.append(pltpu.make_async_copy(q_s, q_hbm, store_sem.at[1]))
+    stores[1].start()
+
     for copy in sends:
         copy.wait_recv()
     step = jnp.exp(-rate_r[chunk(me), :] * float(tok))
@@ -326,7 +336,7 @@
         peer = lax.rem(me + d, n)
         copy = pltpu.make_async_remote_copy(
             src_ref=pref.at[chunk(peer)],
-            dst_ref=inc.at[chunk(me)],
+            dst_ref=inc_hbm.at[chunk(me)],
             send_sem=s2_sem.at[d],
             recv_sem=r2_sem.at[d],
             device_id={"seq": peer},
@@ -334,9 +344,14 @@
         )
         copy.start()
         returns.append(copy)
-    inc[chunk(me), :] = pref[chunk(me), :]
+    stores.append(
+        pltpu.make_async_copy(pref.at[chunk(me)], inc_hbm.at[chunk(me)], store_sem.at[2])
+    )
+    stores[2].start()
     for b in range(rows // modes):
-        end_ref[:, b * LANES : (b + 1) * LANES] = state[b * modes : (b + 1) * modes]
+        end_v[:, b * LANES : (b + 1) * LANES] = state[b * modes : (b + 1) * modes]
+    stores.append(pltpu.make_async_copy(end_v, end_hbm, store_sem.at[3]))
+    stores[3].start()
 
     loads[5].wait()
     vocab = emb_v.shape[0]
@@ -346,52 +361,95 @@
 
     def embed(b, _):
         cols = pl.ds(pl.multiple_of(b * wide, wide), wide)
-        g_s[:, cols] = lax.dot_general(
+        embedded = lax.dot_general(
             one_hot, emb_v[:, cols], (((0,), (0,)), ((), ())),
             preferred_element_type=jnp.float32,
         )
+        for i in range(2):
+            part = pl.ds(pl.multiple_of((b * 2 + i) * LANES, LANES), LANES)
+            filtered = f_s[pl.ds(pl.multiple_of((b * 2 + i) * pitch, SUBL), tok), :]
+            base_v[:, part] = (
+                embedded[:, i * LANES : (i + 1) * LANES] + q_s[:, part] * filtered
+            )
         return 0
 
     lax.fori_loop(0, chans // wide, embed, 0)
-
-    for copy in returns:
-        copy.wait_recv()
-    inc[...] = res_r[...] * inc[...]
-    shares = per_mode(inc)
-    stores = []
-    for h in range(halves):
-        half_poles = poles[h * modes : (h + 1) * modes]
-
-        def carried(t, share, h=h, half_poles=half_poles):
-            share = tuple(p * s for p, s in zip(half_poles, share))
-            terms = list(share)
-            while len(terms) > 1:
-                terms = [a + b for a, b in zip(terms[::2], terms[1::2])]
-            spot = pl.ds(h * SUBL * pitch + t, SUBL, stride=pitch)
-            f_s[spot, :] = f_s[spot, :] + terms[0]
-            return share
-
-        lax.fori_loop(
-            0, tok, carried, tuple(shares[h * modes : (h + 1) * modes]), unroll=8
-        )
-
-        def finish(b, _):
-            cols = pl.ds(pl.multiple_of(b * LANES, LANES), LANES)
-            filtered = f_s[pl.ds(pl.multiple_of(b * pitch, SUBL), tok), :]
-            q_feat = q_s[pl.ds(pl.multiple_of(b * tok, SUBL), tok), :]
-            out_v[:, cols] = (g_s[:, cols] + q_feat * filtered).astype(jnp.bfloat16)
-            return 0
-
-        lax.fori_loop(h * SUBL, (h + 1) * SUBL, finish, 0)
-        span = pl.ds(h * half_cols, half_cols)
-        store = pltpu.make_async_copy(out_v.at[:, span], out_hbm.at[:, span], out_sem.at[h])
-        store.start()
-        stores.append(store)
+    stores.append(pltpu.make_async_copy(base_v, base_hbm, store_sem.at[4]))
+    stores[4].start()
+
     tail_copy.wait_send()
     for copy in returns:
         copy.wait_send()
     for store in stores:
         store.wait()
+    for copy in returns:
+        copy.wait_recv()
+
+
+def finish_kernel(
+    inc_hbm, table_hbm, q_hbm, base_hbm, end_hbm,
+    out_hbm, end_out,
+    inc, table_v, q_v, base_v, end_v, f_s, out_v,
+    load_sem, store_sem,
+):
+    tok, chans = q_v.shape
+    blocks = chans // LANES
+    halves = blocks // SUBL
+    pitch = tok + SUBL
+    modes = SUBL
+    half_cols = SUBL * LANES
+    loads = [
+        pltpu.make_async_copy(src, dst, load_sem.at[i])
+        for i, (src, dst) in enumerate(
+            (
+                (inc_hbm, inc),
+                (table_hbm, table_v),
+                (end_hbm, end_v),
+                (q_hbm, q_v),
+                (base_hbm, base_v),
+            )
+        )
+    ]
+    for load in loads:
+        load.start()
+    for load in loads[:2]:
+        load.wait()
+    inc[...] = table_v[1] * inc[...]
+    stores = []
+    for h in range(halves):
+        spots = [pl.ds(h * SUBL * modes + m, SUBL, stride=modes) for m in range(modes)]
+        poles = [table_v.at[0][spot, :] for spot in spots]
+        shares = tuple(inc[spot, :] for spot in spots)
+
+        def carried(t, share, h=h, poles=poles):
+            share = tuple(p * s for p, s in zip(poles, share))
+            terms = list(share)
+            while len(terms) > 1:
+                terms = [a + b for a, b in zip(terms[::2], terms[1::2])]
+            f_s[pl.ds(h * SUBL * pitch + t, SUBL, stride=pitch), :] = terms[0]
+            return share
+
+        lax.fori_loop(0, tok, carried, shares, unroll=8)
+        if h == 0:
+            loads[2].wait()
+            stores.append(pltpu.make_async_copy(end_v, end_out, store_sem.at[halves]))
+            stores[0].start()
+            loads[3].wait()
+            loads[4].wait()
+
+        def finish(b, _):
+            cols = pl.ds(pl.multiple_of(b * LANES, LANES), LANES)
+            filtered = f_s[pl.ds(pl.multiple_of(b * pitch, SUBL), tok), :]
+            out_v[:, cols] = (base_v[:, cols] + q_v[:, cols] * filtered).astype(jnp.bfloat16)
+            return 0
+
+        lax.fori_loop(h * SUBL, (h + 1) * SUBL, finish, 0)
+        span = pl.ds(h * half_cols, half_cols)
+        store = pltpu.make_async_copy(out_v.at[:, span], out_hbm.at[:, span], store_sem.at[h])
+        store.start()
+        stores.append(store)
+    for store in stores:
+        store.wait()
 
 
 def fused_body(token_ids, embed_table, hyena_qkv, conv_weights, decay_rates, residues, prior_state):
@@ -399,9 +457,13 @@
     members, tok, chans = hyena_qkv.shape
     modes = decay_rates.shape[0]
     blocks = chans // LANES
-    table = pltpu.VMEM((blocks * modes, LANES), jnp.float32)
     f32 = jnp.float32
-    padded = blocks * (tok + SUBL)
+    rows = blocks * modes
+    table = pltpu.VMEM((rows, LANES), f32)
+    padded = pltpu.VMEM((blocks * (tok + SUBL), LANES), f32)
+    whole = pltpu.VMEM((tok, chans), f32)
+    packed = (members * blocks * 2, LANES)
+    end_shape = (modes, chans // n)
     scratch = [
         pltpu.VMEM(hyena_qkv.shape, jnp.bfloat16),
         pltpu.VMEM(embed_table.shape, jnp.bfloat16),
@@ -409,39 +471,63 @@
         pltpu.VMEM(decay_rates.shape, f32),
         pltpu.VMEM(residues.shape, f32),
         pltpu.VMEM(prior_state.shape, f32),
-        pltpu.VMEM((tok, chans), jnp.bfloat16),
-        pltpu.VMEM((members * blocks * 2, LANES), f32),
-        pltpu.VMEM((members * blocks * 2, LANES), jnp.bfloat16),
-        pltpu.VMEM((members * blocks * 2, LANES), jnp.bfloat16),
+        pltpu.VMEM(packed, f32),
+        pltpu.VMEM(packed, jnp.bfloat16),
+        pltpu.VMEM(packed, jnp.bfloat16),
         pltpu.VMEM((members, tok + SUBL, LANES), f32),
-        pltpu.VMEM((blocks * tok, LANES), f32),
-        pltpu.VMEM((padded, LANES), f32),
-        pltpu.VMEM((padded, LANES), f32),
-        pltpu.VMEM((tok, chans), f32),
-    ] + [table] * 10 + [
+        whole,
+        padded,
+        padded,
+        whole,
+        pltpu.VMEM(end_shape, f32),
+        pltpu.VMEM((2, rows, LANES), f32),
+    ] + [table] * 7 + [
         pltpu.SemaphoreType.DMA((6,)),
         pltpu.SemaphoreType.DMA((2,)),
-    ] + [pltpu.SemaphoreType.DMA((n,))] * 4 + [
-        pltpu.SemaphoreType.DMA((blocks // SUBL,)),
-    ]
-    any_spec = pl.BlockSpec(memory_space=pl.ANY)
+    ] + [pltpu.SemaphoreType.DMA((n,))] * 4 + [pltpu.SemaphoreType.DMA((5,))]
+    hbm_spec = pl.BlockSpec(memory_space=pltpu.HBM)
     vmem_spec = pl.BlockSpec(memory_space=pltpu.VMEM)
-    return pl.pallas_call(
+    room = 60 * 1024 * 1024
+    parts = pl.pallas_call(
         functools.partial(fused_kernel, n),
         out_shape=(
-            jax.ShapeDtypeStruct((tok, chans), jnp.bfloat16),
-            jax.ShapeDtypeStruct((modes, chans // n), f32),
+            jax.ShapeDtypeStruct((rows, LANES), f32),
+            jax.ShapeDtypeStruct((2, rows, LANES), f32),
+            jax.ShapeDtypeStruct((tok, chans), f32),
+            jax.ShapeDtypeStruct((tok, chans), f32),
+            jax.ShapeDtypeStruct(end_shape, f32),
         ),
-        in_specs=[vmem_spec] + [any_spec] * 6,
-        out_specs=(any_spec, vmem_spec),
+        in_specs=[vmem_spec] + [hbm_spec] * 6,
+        out_specs=(hbm_spec,) * 5,
         scratch_shapes=scratch,
         compiler_params=pltpu.CompilerParams(
-            collective_id=0, has_side_effects=True, vmem_limit_bytes=40 * 1024 * 1024
+            collective_id=0, has_side_effects=True, vmem_limit_bytes=room
         ),
     )(
         token_ids.reshape(1, tok), embed_table, hyena_qkv, conv_weights,
         decay_rates, residues, prior_state,
     )
+    return pl.pallas_call(
+        finish_kernel,
+        out_shape=(
+            jax.ShapeDtypeStruct((tok, chans), jnp.bfloat16),
+            jax.ShapeDtypeStruct(end_shape, f32),
+        ),
+        in_specs=[hbm_spec] * 5,
+        out_specs=(hbm_spec,) * 2,
+        scratch_shapes=[
+            table,
+            pltpu.VMEM((2, rows, LANES), f32),
+            whole,
+            whole,
+            pltpu.VMEM(end_shape, f32),
+            padded,
+            pltpu.VMEM((tok, chans), jnp.bfloat16),
+            pltpu.SemaphoreType.DMA((5,)),
+            pltpu.SemaphoreType.DMA((blocks // SUBL + 1,)),
+        ],
+        compiler_params=pltpu.CompilerParams(vmem_limit_bytes=room),
+    )(*parts)
 
 
 def body(token_ids, embed_table, hyena_qkv, conv_weights, decay_rates, residues, prior_state):

time: 29.3 us -> 23.4 us (0.80)
  local copies, waits for them, and re-layouts: 8.45 us -> 0 us
  Pallas kernels: 19.9 us -> 22.6 us
    unnamed x16 -> x0, local copies, waits for them, and re-layouts: 8.45 us -> none
    pallas_call x0 -> x1, Pallas kernels: none -> 3.17 us  [fused_body(): pl.pallas_call(finish_kernel, out_shape=(jax.ShapeDtypeStruct((tok, chans...]
    pallas_call x1, Pallas kernels: 19.9 us -> 19.4 us  [fused_body(): pl.pallas_call(functools.partial(fused_kernel, n), out_shape=(jax.ShapeDt...]
where the time goes in v2:
time: 23.4 us; the launch traced here: 23.3 us
  Pallas kernels  22.6 us (97%)
  between operations  0.64 us (3%)
    pallas_call x1, Pallas kernels, fused_body(): pl.pallas_call(functools.partial(fused_kernel, n), out_shape=(jax.ShapeDt...  19.4 us
    pallas_call x1, Pallas kernels, fused_body(): pl.pallas_call(finish_kernel, out_shape=(jax.ShapeDtypeStruct((tok, chans...  3.17 us

profile of v2, /device:TPU:0, one launch (start us, length us, event | category | flops | bytes accessed | tf_op | source)
XLA Modules:
  0.0 23.3 jit_solution(204601771907161303)
XLA Ops:
  0.6 19.4 %shard_map.86 = (f32[128,128]{1,0:T(8,128)}, f32[2,128,128]{2,1,0:T(8,128)}, f32[128,2048]{1,0:T(8,128)}, f32[128,2048]{1,0:T(8,128)}, f32[8,256]{1,0:T(8,128)}) custom-call(s32[1,128]{1,0:T(1,128)} %bitcast.1, bf16[512,2048]{1,0:T(8,128)(2,1)} %emb_hbm.1, bf16[3,128,2048]{2,1,0:T(8,128)(2,1)} %qkv_hbm.1, f32[3,3,2048]{2,1,0:T(4,128)} %cw_hbm.1, ...), custom_call_target="tpu_custom_call" | custom-call | tf_op jit(solution)/shard_map/pallas_call | solution.py:491
  20.1 3.2 %shard_map.87 = (bf16[128,2048]{1,0:T(8,128)(2,1)}, f32[8,256]{1,0:T(8,128)}) custom-call(f32[128,128]{1,0:T(8,128)} %get-tuple-element.7.inc_hbm, f32[2,128,128]{2,1,0:T(8,128)} %get-tuple-element.8.table_hbm, f32[128,2048]{1,0:T(8,128)} %get-tuple-element.9.q_hbm, f32[128,2048]{1,0:T(8,128)} %get-tuple-element.10.base_hbm, f32[8,256]{1,0:T(8,128)} %get-tuple-element.11.end_hbm), custom_call_target="tpu_custom_call" | custom-call | tf_op jit(solution)/shard_map/pallas_call | solution.py:510

commit v3 on v2

--- a/solution.py
+++ b/solution.py
@@ -137,6 +137,12 @@
     rows = blocks // n * modes
     me = lax.axis_index("seq")
 
+    barrier = pltpu.get_barrier_semaphore()
+    for d in range(1, n):
+        pl.semaphore_signal(
+            barrier, inc=1, device_id={"seq": lax.rem(me + d, n)}, device_id_type=MESH
+        )
+
     loads = [
         pltpu.make_async_copy(src, dst, load_sem.at[i])
         for i, (src, dst) in enumerate(
@@ -153,12 +159,6 @@
     for load in loads:
         load.start()
 
-    barrier = pltpu.get_barrier_semaphore()
-    for d in range(1, n):
-        pl.semaphore_signal(
-            barrier, inc=1, device_id={"seq": lax.rem(me + d, n)}, device_id_type=MESH
-        )
-
     loads[0].wait()
 
     def pack_tail(b, _):
@@ -166,6 +166,10 @@
         for m in range(members):
             last = qkv_v[m, tok - 16 : tok, cols].astype(jnp.float32)
             tail32[pl.ds((m * blocks + b) * 2, 2), :] = last[14:16]
+            if m > 0:
+                at = b * 2 * modes + modes + (m - 1) * 4
+                ends[pl.ds(at, 2), :] = qkv_v[m, 0:16, cols].astype(jnp.float32)[0:2]
+                ends[pl.ds(at + 2, 2), :] = last[14:16]
         return 0
 
     lax.fori_loop(0, blocks, pack_tail, 0, unroll=4)
@@ -243,9 +247,32 @@
     zeros = tuple(jnp.zeros((SUBL, LANES), jnp.float32) for _ in range(halves * modes))
     late = lax.fori_loop(2, tok, horner, zeros, unroll=6)
 
+    gains = per_mode(gain_r)
     for i, s in enumerate(late):
         h, m = divmod(i, modes)
-        ends[pl.ds(h * SUBL * modes + m, SUBL, stride=modes), :] = s
+        ends[pl.ds(h * SUBL * 2 * modes + m, SUBL, stride=2 * modes), :] = gains[i] * s
+
+    def chunk(index):
+        return pl.ds(pl.multiple_of(index * rows, SUBL), rows)
+
+    def wide_chunk(index):
+        return pl.ds(pl.multiple_of(index * rows * 2, SUBL), rows * 2)
+
+    sends = []
+    for d in range(1, n):
+        peer = lax.rem(me + d, n)
+        copy = pltpu.make_async_remote_copy(
+            src_ref=ends.at[wide_chunk(peer)],
+            dst_ref=gath.at[wide_chunk(me)],
+            send_sem=s1_sem.at[d],
+            recv_sem=r1_sem.at[d],
+            device_id={"seq": peer},
+            device_id_type=MESH,
+        )
+        copy.start()
+        sends.append(copy)
+    gath[wide_chunk(me), :] = ends[wide_chunk(me), :]
+
     tail_copy.wait_recv()
     tail32[...] = jnp.where(me > 0, tail_recv[...].astype(jnp.float32), 0.0)
 
@@ -266,37 +293,6 @@
         return 0
 
     lax.fori_loop(0, blocks, patch, 0, unroll=2)
-    first, second = tokens(p_s, 0), tokens(p_s, 1)
-    lag = jnp.exp(-rate_r[...] * float(tok - 2))
-    pref[0 : blocks * modes, :] = lag
-    lags = per_mode(pref)
-    gains = per_mode(gain_r)
-    olds = per_mode(ends)
-    for i in range(halves * modes):
-        h, m = divmod(i, modes)
-        early = poles[i] * first[h] + second[h]
-        ends[pl.ds(h * SUBL * modes + m, SUBL, stride=modes), :] = gains[i] * (
-            lags[i] * early + olds[i]
-        )
-
-    def chunk(index):
-        return pl.ds(pl.multiple_of(index * rows, SUBL), rows)
-
-    sends = []
-    for d in range(1, n):
-        peer = lax.rem(me + d, n)
-        copy = pltpu.make_async_remote_copy(
-            src_ref=ends.at[chunk(peer)],
-            dst_ref=gath.at[chunk(me)],
-            send_sem=s1_sem.at[d],
-            recv_sem=r1_sem.at[d],
-            device_id={"seq": peer},
-            device_id_type=MESH,
-        )
-        copy.start()
-        sends.append(copy)
-    gath[chunk(me), :] = ends[chunk(me), :]
-
     weights = per_mode(rg_r)
 
     def scan(t, state):
@@ -323,13 +319,39 @@
 
     for copy in sends:
         copy.wait_recv()
-    step = jnp.exp(-rate_r[chunk(me), :] * float(tok))
-    state = prior_r[chunk(me), :]
     for copy in sends:
         copy.wait_send()
-    for i in range(n):
-        pref[i * rows : (i + 1) * rows, :] = state
-        state = step * state + gath[i * rows : (i + 1) * rows, :]
+    states = []
+    none = jnp.zeros((1, LANES), jnp.float32)
+    for c in range(rows // modes):
+        block = me * (rows // modes) + c
+        own = pl.ds(pl.multiple_of(block * modes, SUBL), modes)
+        cols = pl.ds(pl.multiple_of(block * LANES, LANES), LANES)
+        rate_c = rate_r[own, :]
+        step = jnp.exp(-rate_c * float(tok))
+        late_gain = gain_r[own, :] * jnp.exp(-rate_c * float(tok - 2))
+        pole_c = table_v[0, own, :]
+        filters = [taps(m, cols) for m in (1, 2)]
+        state = prior_r[own, :]
+        tails = [(none, none), (none, none)]
+        for i in range(n):
+            pref[i * rows + c * modes : i * rows + (c + 1) * modes, :] = state
+            at = i * rows * 2 + c * modes * 2
+            feats = []
+            for m in range(2):
+                x0, x1, y0, y1 = [
+                    gath[at + modes + m * 4 + r : at + modes + m * 4 + r + 1, :]
+                    for r in range(4)
+                ]
+                w0, w1, w2 = filters[m]
+                t0, t1 = tails[m]
+                feats.append(
+                    (w0 * x0 + w1 * t1 + w2 * t0, w0 * x1 + w1 * x0 + w2 * t1)
+                )
+                tails[m] = (y0, y1)
+            early = pole_c * (feats[0][0] * feats[1][0]) + feats[0][1] * feats[1][1]
+            state = step * state + (gath[at : at + modes, :] + late_gain * early)
+        states.append(state)
 
     returns = []
     for d in range(1, n):
@@ -349,7 +371,7 @@
     )
     stores[2].start()
     for b in range(rows // modes):
-        end_v[:, b * LANES : (b + 1) * LANES] = state[b * modes : (b + 1) * modes]
+        end_v[:, b * LANES : (b + 1) * LANES] = states[b]
     stores.append(pltpu.make_async_copy(end_v, end_hbm, store_sem.at[3]))
     stores[3].start()
 
@@ -481,7 +503,11 @@
         whole,
         pltpu.VMEM(end_shape, f32),
         pltpu.VMEM((2, rows, LANES), f32),
-    ] + [table] * 7 + [
+    ] + [table] * 4 + [
+        pltpu.VMEM((2 * rows, LANES), f32),
+        pltpu.VMEM((2 * rows, LANES), f32),
+        table,
+    ] + [
         pltpu.SemaphoreType.DMA((6,)),
         pltpu.SemaphoreType.DMA((2,)),
     ] + [pltpu.SemaphoreType.DMA((n,))] * 4 + [pltpu.SemaphoreType.DMA((5,))]

time: 23.4 us -> 22 us (0.940)
  Pallas kernels: 22.6 us -> 21.2 us
    pallas_call x1, Pallas kernels: 19.4 us -> 18 us  [fused_body(): pl.pallas_call(functools.partial(fused_kernel, n), out_shape=(jax.ShapeDt...]
where the time goes in v3:
time: 22 us; the launch traced here: 21.8 us
  Pallas kernels  21.2 us (96%)
  between operations  0.64 us (3%)
    pallas_call x1, Pallas kernels, fused_body(): pl.pallas_call(functools.partial(fused_kernel, n), out_shape=(jax.ShapeDt...  18 us
    pallas_call x1, Pallas kernels, fused_body(): pl.pallas_call(finish_kernel, out_shape=(jax.ShapeDtypeStruct((tok, chans...  3.17 us

profile of v3, /device:TPU:0, one launch (start us, length us, event | category | flops | bytes accessed | tf_op | source)
XLA Modules:
  0.0 21.8 jit_solution(3685616191583840422)
XLA Ops:
  0.6 18.0 %shard_map.86 = (f32[128,128]{1,0:T(8,128)}, f32[2,128,128]{2,1,0:T(8,128)}, f32[128,2048]{1,0:T(8,128)}, f32[128,2048]{1,0:T(8,128)}, f32[8,256]{1,0:T(8,128)}) custom-call(s32[1,128]{1,0:T(1,128)} %bitcast.1, bf16[512,2048]{1,0:T(8,128)(2,1)} %emb_hbm.1, bf16[3,128,2048]{2,1,0:T(8,128)(2,1)} %qkv_hbm.1, f32[3,3,2048]{2,1,0:T(4,128)} %cw_hbm.1, ...), custom_call_target="tpu_custom_call" | custom-call | tf_op jit(solution)/shard_map/pallas_call | solution.py:517
  18.6 3.2 %shard_map.87 = (bf16[128,2048]{1,0:T(8,128)(2,1)}, f32[8,256]{1,0:T(8,128)}) custom-call(f32[128,128]{1,0:T(8,128)} %get-tuple-element.7.inc_hbm, f32[2,128,128]{2,1,0:T(8,128)} %get-tuple-element.8.table_hbm, f32[128,2048]{1,0:T(8,128)} %get-tuple-element.9.q_hbm, f32[128,2048]{1,0:T(8,128)} %get-tuple-element.10.base_hbm, f32[8,256]{1,0:T(8,128)} %get-tuple-element.11.end_hbm), custom_call_target="tpu_custom_call" | custom-call | tf_op jit(solution)/shard_map/pallas_call | solution.py:536

commit v4 on v3

--- a/solution.py
+++ b/solution.py
@@ -172,7 +172,7 @@
                 ends[pl.ds(at + 2, 2), :] = last[14:16]
         return 0
 
-    lax.fori_loop(0, blocks, pack_tail, 0, unroll=4)
+    lax.fori_loop(0, blocks, pack_tail, 0, unroll=8)
     tail_send[...] = tail32[...].astype(jnp.bfloat16)
     pl.semaphore_wait(barrier, n - 1)
     tail_copy = pltpu.make_async_remote_copy(
@@ -226,7 +226,7 @@
         p_s[pl.ds(pl.multiple_of(b * pitch, SUBL), tok), :] = k_feat * v_feat
         return 0
 
-    lax.fori_loop(0, blocks, short, 0)
+    lax.fori_loop(0, blocks, short, 0, unroll=2)
 
     def per_mode(ref):
         return [
@@ -245,7 +245,7 @@
         return tuple(poles[i] * s + now[i // modes] for i, s in enumerate(state))
 
     zeros = tuple(jnp.zeros((SUBL, LANES), jnp.float32) for _ in range(halves * modes))
-    late = lax.fori_loop(2, tok, horner, zeros, unroll=6)
+    late = lax.fori_loop(2, tok, horner, zeros, unroll=14)
 
     gains = per_mode(gain_r)
     for i, s in enumerate(late):
@@ -454,7 +454,7 @@
         lax.fori_loop(0, tok, carried, shares, unroll=8)
         if h == 0:
             loads[2].wait()
-            stores.append(pltpu.make_async_copy(end_v, end_out, store_sem.at[halves]))
+            stores.append(pltpu.make_async_copy(end_v, end_out, store_sem.at[2 * halves]))
             stores[0].start()
             loads[3].wait()
             loads[4].wait()
@@ -465,11 +465,14 @@
             out_v[:, cols] = (base_v[:, cols] + q_v[:, cols] * filtered).astype(jnp.bfloat16)
             return 0
 
-        lax.fori_loop(h * SUBL, (h + 1) * SUBL, finish, 0)
-        span = pl.ds(h * half_cols, half_cols)
-        store = pltpu.make_async_copy(out_v.at[:, span], out_hbm.at[:, span], store_sem.at[h])
-        store.start()
-        stores.append(store)
+        for part in range(2 * h, 2 * h + 2):
+            lax.fori_loop(part * SUBL // 2, (part + 1) * SUBL // 2, finish, 0, unroll=2)
+            span = pl.ds(part * half_cols // 2, half_cols // 2)
+            store = pltpu.make_async_copy(
+                out_v.at[:, span], out_hbm.at[:, span], store_sem.at[part]
+            )
+            store.start()
+            stores.append(store)
     for store in stores:
         store.wait()
 
@@ -550,7 +553,7 @@
             padded,
             pltpu.VMEM((tok, chans), jnp.bfloat16),
             pltpu.SemaphoreType.DMA((5,)),
-            pltpu.SemaphoreType.DMA((blocks // SUBL + 1,)),
+            pltpu.SemaphoreType.DMA((2 * (blocks // SUBL) + 1,)),
         ],
         compiler_params=pltpu.CompilerParams(vmem_limit_bytes=room),
     )(*parts)

time: 22 us -> 21.8 us (level)
  no operation moved by 1% of the time
where the time goes in v4:
time: 21.8 us; the launch traced here: 21.7 us
  Pallas kernels  21 us (96%)
  between operations  0.64 us (3%)
    pallas_call x1, Pallas kernels, fused_body(): pl.pallas_call(functools.partial(fused_kernel, n), out_shape=(jax.ShapeDt...  17.9 us
    pallas_call x1, Pallas kernels, fused_body(): pl.pallas_call(finish_kernel, out_shape=(jax.ShapeDtypeStruct((tok, chans...  3.15 us

profile of v4, /device:TPU:0, one launch (start us, length us, event | category | flops | bytes accessed | tf_op | source)
XLA Modules:
  0.0 21.7 jit_solution(18150782167421301109)
XLA Ops:
  0.6 17.9 %shard_map.86 = (f32[128,128]{1,0:T(8,128)}, f32[2,128,128]{2,1,0:T(8,128)}, f32[128,2048]{1,0:T(8,128)}, f32[128,2048]{1,0:T(8,128)}, f32[8,256]{1,0:T(8,128)}) custom-call(s32[1,128]{1,0:T(1,128)} %bitcast.1, bf16[512,2048]{1,0:T(8,128)(2,1)} %emb_hbm.1, bf16[3,128,2048]{2,1,0:T(8,128)(2,1)} %qkv_hbm.1, f32[3,3,2048]{2,1,0:T(4,128)} %cw_hbm.1, ...), custom_call_target="tpu_custom_call" | custom-call | tf_op jit(solution)/shard_map/pallas_call | solution.py:520
  18.5 3.2 %shard_map.87 = (bf16[128,2048]{1,0:T(8,128)(2,1)}, f32[8,256]{1,0:T(8,128)}) custom-call(f32[128,128]{1,0:T(8,128)} %get-tuple-element.7.inc_hbm, f32[2,128,128]{2,1,0:T(8,128)} %get-tuple-element.8.table_hbm, f32[128,2048]{1,0:T(8,128)} %get-tuple-element.9.q_hbm, f32[128,2048]{1,0:T(8,128)} %get-tuple-element.10.base_hbm, f32[8,256]{1,0:T(8,128)} %get-tuple-element.11.end_hbm), custom_call_target="tpu_custom_call" | custom-call | tf_op jit(solution)/shard_map/pallas_call | solution.py:539
